TPU v7x, 32 devices: a whole 2x2x4 slice. The times are simulated.
32 devices in a mesh: agg: 8 (over y, x, core), grp: 4 (over z).
Axes of the slice: x: 2, y: 2, z: 4, core: 2. Of those that a mesh axis runs over, the one named last changes fastest.
Arguments:
- a_blocks: bfloat16 [8, 4, 16, 5, 128, 128], P('agg', 'grp'), may hold values from -0.5 to 0.5
- a_cols: int32 [8, 4, 16, 5], P('agg', 'grp'), may hold values from 0 to 23, as said below
- p_blocks: bfloat16 [8, 4, 16, 2, 128, 128], P('agg', 'grp'), may hold values from -0.5 to 0.5
- p_cols: int32 [8, 4, 16, 2], P(None, 'grp'), may hold values from 0 to 2, as said below
Outputs:
- coarse_matrix: bfloat16 [8, 128, 3, 9, 128], P('agg')
Inputs may be any that keep to these rules, and one draw needn't show every extreme that they name: `a_cols`: slot 0 of row r is 4 + r. In every region but the first, slot 1 of the rows r < 4 names a row 0 to 4 - 1 (row 0 names 0); in every region but the last, slot 4 of the rows r >= 12 names a row 20 to 16 + 2 * 4 - 1 (row 15 names the last). All other slots name rows 4 to 19; a row may name a column more than once. `p_cols`: the 2 entries of a row are 2 consecutive coarse rows counted modulo 3, all different. Every index of agg holds the whole array.
All inputs are finite; a program needn't handle non-finite values.
Results may differ from a plain program's by a relative error of at most 0.025.
Values may be sent and summed in bfloat16 or wider, within the bound.
A program may use at most 64 MiB of HBM per device.

v0:
```python
import jax
import jax.numpy as jnp
from jax import lax
from jax.sharding import PartitionSpec as P

NC = 3
HB = 4


def with_halo(block, sides, width):
    for axis, dim in sides:
        count = lax.axis_size(axis)
        forward = [(i, i + 1) for i in range(count - 1)]
        backward = [(target, source) for source, target in forward]
        low = lax.ppermute(
            lax.slice_in_dim(block, block.shape[dim] - width, None, axis=dim), axis, forward
        )
        high = lax.ppermute(lax.slice_in_dim(block, 0, width, axis=dim), axis, backward)
        block = jnp.concatenate([low, block, high], axis=dim)
    return block


def body(a_blocks, a_cols, p_blocks, p_cols):
    a_local = a_blocks[0, 0]
    col_local = a_cols[0, 0]
    p_local = p_blocks[0, 0]
    row_count, a_slots = col_local.shape
    p_slots = p_local.shape[1]
    width = p_local.shape[-1]
    band = 3 * NC
    group_rows = 4
    group_count = row_count // group_rows
    region = lax.axis_index("agg")
    last_region = lax.axis_size("agg") - 1
    p_extended = with_halo(p_local, (("agg", 0),), HB)
    pattern = p_cols[:, 0]

    def region_ids(index):
        return lax.dynamic_index_in_dim(pattern, index, 0, keepdims=False)

    pattern_own = region_ids(region)
    ids_extended = jnp.concatenate(
        [
            region_ids(jnp.maximum(region - 1, 0))[row_count - HB :],
            pattern_own + NC,
            region_ids(jnp.minimum(region + 1, last_region))[:HB] + 2 * NC,
        ],
        0,
    )
    slot_ids = ids_extended[col_local].reshape(row_count, a_slots * p_slots)

    def product_group(inputs):
        a_group, col_group = inputs
        taken = p_extended[col_group]
        result = jnp.einsum("rkxy,rkmyz->rkmxz", a_group, taken, preferred_element_type=jnp.float32)
        return result.astype(jnp.bfloat16).reshape(group_rows, a_slots * p_slots, width, width)

    applied = lax.map(
        product_group,
        (
            a_local.reshape(group_count, group_rows, a_slots, width, width),
            col_local.reshape(group_count, group_rows, a_slots),
        ),
    )
    applied = applied.reshape(row_count, a_slots * p_slots, width, width)
    band_mask = (slot_ids[:, :, None] == jnp.arange(band, dtype=jnp.int32)[None, None, :]).astype(
        jnp.bfloat16
    )
    grouped = jnp.einsum("rsd,rsxz->rdxz", band_mask, applied, preferred_element_type=jnp.float32)
    grouped_high = grouped.astype(jnp.bfloat16)
    grouped_low = (grouped - grouped_high.astype(jnp.float32)).astype(jnp.bfloat16)
    coarse_mask = (
        pattern_own[:, :, None] == jnp.arange(NC, dtype=jnp.int32)[None, None, :]
    ).astype(jnp.bfloat16)
    p_routed = jnp.einsum(
        "rnc,rnxy->rcxy", coarse_mask, p_local, preferred_element_type=jnp.float32
    ).astype(jnp.bfloat16)
    term = jnp.einsum("rcxy,rdxz->ycdz", p_routed, grouped_high, preferred_element_type=jnp.float32)
    term = term + jnp.einsum(
        "rcxy,rdxz->ycdz", p_routed, grouped_low, preferred_element_type=jnp.float32
    )
    summed = lax.psum(term.astype(jnp.bfloat16), "grp")
    return summed.reshape(1, width, NC, band, width)


def solution(mesh):
    return jax.shard_map(
        body,
        mesh=mesh,
        in_specs=(
            P("agg", "grp", None, None, None, None),
            P("agg", "grp", None, None),
            P("agg", "grp", None, None, None, None),
            P(None, "grp", None, None),
        ),
        out_specs=P("agg", None, None, None, None),
        check_vma=False,
    )
```

profile of v0, /device:TPU:0, one launch (start us, length us, event | category | flops | bytes accessed | tf_op | source)
XLA Modules:
  0.0 126.1 jit_solution(13967826049136949899)
XLA Ops:
  6.5 1.1 slice_bitcast_fusion.1
  7.6 2.4 %collective-permute-start = (bf16[4,2,128,128]{3,2,1,0:T(8,128)(2,1)S(1)}, bf16[4,2,128,128]{3,2,1,0:T(8,128)(2,1)S(1)}, u32[]{:S(2)}, u32[]{:S(2)}) collective-permute-start(bf16[4,2,128,128]{3,2,1,0:T(8,128)(2,1)S(1)} %get-tuple-element.65), channel_id=1, source_target_pairs={{0,4},{4,8},{8,12},{12,16},{16,20},{20,24},{24,28},{1,5},{5,9},{9,... | collective-permute-start | bytes 786440 | tf_op jit(solution)/shard_map/ppermute | solution.py:15
  10.0 1.3 %collective-permute-start.1 = (bf16[4,2,128,128]{3,2,1,0:T(8,128)(2,1)S(1)}, bf16[4,2,128,128]{3,2,1,0:T(8,128)(2,1)S(1)}, u32[]{:S(2)}, u32[]{:S(2)}) collective-permute-start(bf16[4,2,128,128]{3,2,1,0:T(8,128)(2,1)S(1)} %get-tuple-element.66), channel_id=1, source_target_pairs={{4,0},{8,4},{12,8},{16,12},{20,16},{24,20},{28,24},{5,1},{9,5},{13... | collective-permute-start | bytes 786440 | tf_op jit(solution)/shard_map/ppermute | solution.py:18
  11.3 0.7 compare_select_fusion.1
  12.0 0.8 copy.68
  12.8 0.7 broadcast_add_fusion
  13.4 0.7 constant_dynamic-slice_fusion.1
  14.3 0.1 copy.47
  14.5 0.1 reshape.91
  14.6 0.6 gather_fusion.1
  15.3 4.4 %fusion.23 = bf16[16,3,128,128]{3,1,2,0:T(4,128)(2,1)} fusion(bf16[16,2,128,128]{3,2,1,0:T(8,128)(2,1)} %bitcast.93, s32[16,2]{1,0:T(8,128)S(1)} %copy.51), kind=kOutput, calls=%fused_computation.26 | convolution fusion | flops 3145824 | bytes 2621568 | tf_op jit(solution)/shard_map/rnc,rnxy->rcxy/dot_general | solution.py:75
  19.7 0.2 pad_maximum_fusion
  19.9 15.0 %while.10 = (s32[]{:T(128)}, bf16[4,4,10,128,128]{3,4,2,1,0:T(8,128)(2,1)}, s32[4,4,5]{2,1,0:T(4,128)S(1)}, bf16[24,2,128,128]{3,2,1,0:T(8,128)(2,1)S(1)}, bf16[4,4,5,128,128]{4,3,2,1,0:T(8,128)(2,1)}, /*index=5*/s32[]{:T(128)}) while((s32[]{:T(128)}, bf16[4,4,10,128,128]{3,4,2,1,0:T(8,128)(2,1)}, s32[4,4,5]{2,1,0:T(4,128)S(1)}, ...), condition=%wide.region_1.2_spmd, body=%wide.region_0.1_spmd.sunk | while | flops 168428608 | bytes 8525353 | solution.py:58
  20.0 0.8 gather_fusion
  20.9 1.6 %convolution_convert_fusion.2 = bf16[4,5,2,128,128]{4,3,2,1,0:T(8,128)(2,1)S(1)} fusion(bf16[4,5,2,128,128]{4,3,2,1,0:T(8,128)(2,1)S(1)} %bitcast.90, bf16[4,4,5,128,128]{4,3,2,1,0:T(8,128)(2,1)} %get-tuple-element.118, s32[]{:T(128)} %get-tuple-element.108), kind=kOutput, calls=%fused_computation.2.clone.1 | convolution fusion | flops 168427520 | bytes 3277312 | tf_op jit(solution)/shard_map/while/body/eval_jaxpr/rkxy,rkmyz->rkmxz/dot_general | solution.py:55
  22.5 1.3 constant_dynamic-update-slice_fusion.2
  23.8 0.1 reshape.114
  23.9 0.8 gather_fusion
  24.7 1.6 %convolution_convert_fusion.2 = bf16[4,5,2,128,128]{4,3,2,1,0:T(8,128)(2,1)S(1)} fusion(bf16[4,5,2,128,128]{4,3,2,1,0:T(8,128)(2,1)S(1)} %bitcast.90, bf16[4,4,5,128,128]{4,3,2,1,0:T(8,128)(2,1)} %get-tuple-element.118, s32[]{:T(128)} %get-tuple-element.108), kind=kOutput, calls=%fused_computation.2.clone.1 | convolution fusion | flops 168427520 | bytes 3277312 | tf_op jit(solution)/shard_map/while/body/eval_jaxpr/rkxy,rkmyz->rkmxz/dot_general | solution.py:55
  26.3 1.2 constant_dynamic-update-slice_fusion.2
  27.6 0.8 gather_fusion
  28.4 1.6 %convolution_convert_fusion.2 = bf16[4,5,2,128,128]{4,3,2,1,0:T(8,128)(2,1)S(1)} fusion(bf16[4,5,2,128,128]{4,3,2,1,0:T(8,128)(2,1)S(1)} %bitcast.90, bf16[4,4,5,128,128]{4,3,2,1,0:T(8,128)(2,1)} %get-tuple-element.118, s32[]{:T(128)} %get-tuple-element.108), kind=kOutput, calls=%fused_computation.2.clone.1 | convolution fusion | flops 168427520 | bytes 3277312 | tf_op jit(solution)/shard_map/while/body/eval_jaxpr/rkxy,rkmyz->rkmxz/dot_general | solution.py:55
  30.0 1.1 constant_dynamic-update-slice_fusion.2
  31.3 0.8 gather_fusion
  32.1 1.6 %convolution_convert_fusion.2 = bf16[4,5,2,128,128]{4,3,2,1,0:T(8,128)(2,1)S(1)} fusion(bf16[4,5,2,128,128]{4,3,2,1,0:T(8,128)(2,1)S(1)} %bitcast.90, bf16[4,4,5,128,128]{4,3,2,1,0:T(8,128)(2,1)} %get-tuple-element.118, s32[]{:T(128)} %get-tuple-element.108), kind=kOutput, calls=%fused_computation.2.clone.1 | convolution fusion | flops 168427520 | bytes 3277312 | tf_op jit(solution)/shard_map/while/body/eval_jaxpr/rkxy,rkmyz->rkmxz/dot_general | solution.py:55
  33.7 1.2 constant_dynamic-update-slice_fusion.2
  34.9 12.8 %copy.49 = bf16[16,10,128,128]{3,1,2,0:T(8,128)(2,1)} copy(bf16[16,10,128,128]{2,3,1,0:T(8,128)(2,1)} %bitcast.91) | data formatting | bytes 10485760 | tf_op jit(solution)/shard_map/reshape | solution.py:65
  47.7 5.8 %fusion.26 = f32[16,9,128,128]{3,1,2,0:T(8,128)S(1)} fusion(bf16[16,10,128,128]{3,1,2,0:T(8,128)(2,1)} %copy.49, s32[16,10]{1,0:T(8,128)S(1)} %eq.28), kind=kOutput, calls=%fused_computation.32 | convolution fusion | flops 47187360 | bytes 14680704 | tf_op jit(solution)/shard_map/rsd,rsxz->rdxz/dot_general | solution.py:69
  53.5 5.0 %fusion.5 = f32[9,128,3,128,1]{3,1,4,2,0:T(8,128)S(1)} fusion(f32[16,9,128,128]{3,1,2,0:T(8,128)S(1)} %fusion.26, bf16[16,3,128,128]{3,1,2,0:T(4,128)(2,1)S(1)} %copy-done.1), kind=kOutput, calls=%fused_computation.13 | convolution fusion | flops 1821376512 | bytes 12779520 | tf_op jit(solution)/shard_map/rcxy,rdxz->ycdz/dot_general | solution.py:79
  58.5 7.0 %fusion.18 = bf16[1,128,3,9,128]{1,4,2,3,0:T(8,128)(2,1)} fusion(f32[9,128,3,128,1]{3,1,4,2,0:T(8,128)S(1)} %fusion.5, f32[16,9,128,128]{3,1,2,0:T(8,128)S(1)} %fusion.26, bf16[16,3,128,128]{3,1,2,0:T(4,128)(2,1)S(1)} %copy-done.1), kind=kOutput, calls=%fused_computation.25 | convolution fusion | flops 1812824064 | bytes 13664256 | tf_op jit(solution)/shard_map/rcxy,rdxz->ycdz/dot_general | solution.py:78
  65.6 51.4 %all-reduce.2.cloned.1.call-done = bf16[1,128,3,9,128]{1,4,2,3,0:T(8,128)(2,1)} async-done(((bf16[1,128,3,9,128]{1,4,2,3,0:T(8,128)(2,1)}), bf16[1,128,3,9,128]{1,4,2,3,0:T(8,128)(2,1)}) %all-reduce.2.cloned.1.call-update) | async-done | bytes 884752 | tf_op jit(solution)/shard_map/psum | solution.py:82
  117.1 2.2 %copy.59 = bf16[1,128,3,9,128]{4,1,3,2,0:T(8,128)(2,1)} copy(bf16[1,128,3,9,128]{1,4,2,3,0:T(8,128)(2,1)} %all-reduce.2.cloned.1.call-done) | data formatting | bytes 1769472 | tf_op jit(solution)/shard_map/psum | solution.py:82
  (26 shorter events, 0.7 us)
Async XLA Ops:
  6.5 110.5 %all-reduce.2.cloned.1.call-start = ((), (), s32[]{:S(2)}) async-start(), calls=%async_computation | async-start | bytes 1769472 | tf_op jit(solution)/shard_map/psum | solution.py:82
  7.6 12.1 %collective-permute-start = (bf16[4,2,128,128]{3,2,1,0:T(8,128)(2,1)S(1)}, bf16[4,2,128,128]{3,2,1,0:T(8,128)(2,1)S(1)}, u32[]{:S(2)}, u32[]{:S(2)}) collective-permute-start(bf16[4,2,128,128]{3,2,1,0:T(8,128)(2,1)S(1)} %get-tuple-element.65), channel_id=1, source_target_pairs={{0,4},{4,8},{8,12},{12,16},{16,20},{20,24},{24,28},{1,5},{5,9},{9,... | collective-permute-start | bytes 786440 | tf_op jit(solution)/shard_map/ppermute | solution.py:15
  10.0 9.7 %collective-permute-start.1 = (bf16[4,2,128,128]{3,2,1,0:T(8,128)(2,1)S(1)}, bf16[4,2,128,128]{3,2,1,0:T(8,128)(2,1)S(1)}, u32[]{:S(2)}, u32[]{:S(2)}) collective-permute-start(bf16[4,2,128,128]{3,2,1,0:T(8,128)(2,1)S(1)} %get-tuple-element.66), channel_id=1, source_target_pairs={{4,0},{8,4},{12,8},{16,12},{20,16},{24,20},{28,24},{5,1},{9,5},{13... | collective-permute-start | bytes 786440 | tf_op jit(solution)/shard_map/ppermute | solution.py:18
  15.3 4.4 %copy-start = (bf16[1,1,16,2,128,128]{5,4,3,2,1,0:T(8,128)(2,1)S(1)}, bf16[1,1,16,2,128,128]{5,4,3,2,1,0:T(8,128)(2,1)}, u32[]{:S(2)}) copy-start(bf16[1,1,16,2,128,128]{5,4,3,2,1,0:T(8,128)(2,1)} %param.8) | copy-start | bytes 3145732
  47.7 5.8 %copy-start.1 = (bf16[16,3,128,128]{3,1,2,0:T(4,128)(2,1)S(1)}, bf16[16,3,128,128]{3,1,2,0:T(4,128)(2,1)}, u32[]{:S(2)}) copy-start(bf16[16,3,128,128]{3,1,2,0:T(4,128)(2,1)} %fusion.23) | copy-start | bytes 4718596
Sparse Core Ops, SparseCore 0:
  65.7 51.2 all-reduce.1
where the time goes:
time: 127 us; the launch traced here: 126 us
  waiting for transfers between devices  51.5 us (41%)
  matrix products  28.8 us (23%)
  local copies, waits for them, and re-layouts  26.8 us (21%)
  between operations  13.5 us (11%)
  starting transfers between devices  3.67 us (3%)
  other arithmetic  1.77 us (1%)
    psum x1, waiting for transfers between devices, body(): summed = lax.psum(term.astype(jnp.bfloat16), 'grp')  51.4 us
    reshape x1, local copies, waits for them, and re-layouts, body(): applied = applied.reshape(row_count, a_slots * p_slots, width, width)  12.8 us
    dot_general x1, matrix products, body(): jnp.einsum('rcxy,rdxz->ycdz', p_routed, grouped_high, preferred_element_t...  7.05 us
    dot_general x4, matrix products, product_group(): jnp.einsum('rkxy,rkmyz->rkmxz', a_group, taken, preferred_element_type=jn...  6.56 us
    dot_general x1, matrix products, body(): jnp.einsum('rsd,rsxz->rdxz', band_mask, applied, preferred_element_type=j...  5.84 us
    dot_general x1, matrix products, body(): jnp.einsum('rcxy,rdxz->ycdz', p_routed, grouped_low, preferred_element_ty...  4.99 us
    dynamic_update_slice x4, local copies, waits for them, and re-layouts, body(): lax.map(product_group, (a_local.reshape(group_count, group_rows, a_slots,...  4.78 us
    dot_general x1, matrix products, body(): jnp.einsum('rnc,rnxy->rcxy', coarse_mask, p_local, preferred_element_type...  4.38 us
  transfers between devices with their start and end apart: 3, of which 1 were waited for; matrix products, arithmetic and copies ran while one was open for 7% of the time, Pallas kernels for 0%

commit v1 on v0

v1 whole, which is shorter than its diff:
```python
import functools

import jax
import jax.numpy as jnp
from jax import lax
from jax.experimental import pallas as pl
from jax.experimental.pallas import tpu as pltpu
from jax.sharding import PartitionSpec as P

NC = 3
HB = 4
LAG = 4
GROUP = 4
MESH = pl.DeviceIdType.MESH
BF = jnp.bfloat16
F32 = jnp.float32


def kernel(
    regions,
    members,
    a_ref,
    ac_ref,
    p_ref,
    pc_ref,
    out_ref,
    a_v,
    p_v,
    halo_lo,
    halo_hi,
    e_own,
    e_lo,
    e_hi,
    et,
    g_own,
    g_lo,
    g_hi,
    term,
    half,
    from_outer,
    from_inner,
    a_sem,
    p_sem,
    lo_send,
    lo_recv,
    hi_send,
    hi_recv,
    up_send,
    up_recv,
    down_send,
    down_recv,
    out_sem,
):
    rows, slots, width = a_v.shape[0], a_v.shape[1], a_v.shape[2]
    wide = NC * width
    band = 3 * NC
    count = NC * band
    region = lax.axis_index("agg")
    g = lax.axis_index("grp")
    first = region == 0
    last = region == regions - 1
    left = g < members // 2
    inner = jnp.where(left, g + 1, g - 1)
    outer = jnp.where(left, g - 1, g + 1)
    has_outer = jnp.logical_and(g > 0, g < members - 1)
    is_end = jnp.logical_not(has_outer)
    is_mid = jnp.logical_or(g == members // 2 - 1, g == members // 2)

    p_copy = pltpu.make_async_copy(p_ref.at[0, 0], p_v, p_sem)
    p_copy.start()

    def a_copy(i):
        return pltpu.make_async_copy(
            a_ref.at[0, 0, pl.ds(i * GROUP, GROUP)],
            a_v.at[pl.ds(i * GROUP, GROUP)],
            a_sem.at[i],
        )

    for i in range(rows // GROUP):
        a_copy(i).start()

    barrier = pltpu.get_barrier_semaphore()

    def greet(there, agg, grp):
        @pl.when(there)
        def _():
            pl.semaphore_signal(barrier, inc=1, device_id=(agg, grp), device_id_type=MESH)

    greet(jnp.logical_not(first), region - 1, g)
    greet(jnp.logical_not(last), region + 1, g)
    greet(has_outer, region, outer)
    greet(jnp.bool_(True), region, inner)
    pl.semaphore_wait(
        barrier,
        1
        + has_outer.astype(jnp.int32)
        + jnp.logical_not(first).astype(jnp.int32)
        + jnp.logical_not(last).astype(jnp.int32),
    )

    def to_next():
        return pltpu.make_async_remote_copy(
            src_ref=p_ref.at[0, 0, pl.ds(rows - HB, HB)],
            dst_ref=halo_lo,
            send_sem=lo_send,
            recv_sem=lo_recv,
            device_id=(region + 1, g),
            device_id_type=MESH,
        )

    def to_previous():
        return pltpu.make_async_remote_copy(
            src_ref=p_ref.at[0, 0, pl.ds(0, HB)],
            dst_ref=halo_hi,
            send_sem=hi_send,
            recv_sem=hi_recv,
            device_id=(region - 1, g),
            device_id_type=MESH,
        )

    @pl.when(jnp.logical_not(last))
    def _():
        to_next().start()

    @pl.when(jnp.logical_not(first))
    def _():
        to_previous().start()

    def placed(block_0, block_1, id_0, id_1):
        zero = jnp.zeros_like(block_0)
        return jnp.concatenate(
            [
                jnp.where(id_0 == c, block_0, jnp.where(id_1 == c, block_1, zero))
                for c in range(NC)
            ],
            axis=1,
        )

    p_copy.wait()

    def build(r, carry):
        row = placed(p_v[r, 0], p_v[r, 1], pc_ref[region, 0, r, 0], pc_ref[region, 0, r, 1])
        e_own[r] = row
        et[:, pl.ds(pl.multiple_of(r * width, width), width)] = row.T
        return carry

    lax.fori_loop(0, rows, build, 0, unroll=4)

    def multiply(i, carry):
        a_copy(i).wait()
        for j in range(GROUP):
            r = i * GROUP + j
            pieces = []
            for k in range(slots):
                col = jnp.clip(ac_ref[0, 0, r, k] - HB, 0, rows - 1)
                piece = e_own[col]
                if k == 1:
                    keep = jnp.logical_or(first, i > 0)
                    piece = jnp.where(keep, piece, jnp.zeros_like(piece))
                if k == slots - 1:
                    keep = jnp.logical_or(last, i < rows // GROUP - 1)
                    piece = jnp.where(keep, piece, jnp.zeros_like(piece))
                pieces.append(piece)
            lhs = jnp.concatenate([a_v[r, k] for k in range(slots)], axis=1)
            rhs = jnp.concatenate(pieces, axis=0)
            res = jnp.dot(lhs, rhs, preferred_element_type=F32)
            g_own[pl.ds(pl.multiple_of(r * width, width), width), :] = res.astype(BF)
        return carry

    lax.fori_loop(0, rows // GROUP, multiply, 0)

    def store_term(part, lhs_cols, rhs):
        for c in range(NC):
            res = jnp.dot(
                et[c * width : (c + 1) * width, lhs_cols], rhs[...], preferred_element_type=F32
            )
            for d in range(NC):
                term[c * band + part * NC + d] = res[:, d * width : (d + 1) * width]

    def block_of(s):
        part = (s // (NC * NC) + 1) % 3
        i = s % (NC * NC)
        return (i // NC) * band + part * NC + i % NC

    def up_copy(b, middle):
        return pltpu.make_async_remote_copy(
            src_ref=half.at[b],
            dst_ref=(from_inner if middle else from_outer).at[b],
            send_sem=up_send.at[b],
            recv_sem=(down_recv if middle else up_recv).at[b],
            device_id=(region, inner),
            device_id_type=MESH,
        )

    def down_copy(b):
        return pltpu.make_async_remote_copy(
            src_ref=from_inner.at[b],
            dst_ref=from_inner.at[b],
            send_sem=down_send.at[b],
            recv_sem=down_recv.at[b],
            device_id=(region, outer),
            device_id_type=MESH,
        )

    def out_copy(b):
        return pltpu.make_async_copy(from_inner.at[b], out_ref.at[b], out_sem.at[b])

    def send_up(b):
        @pl.when(is_mid)
        def _():
            up_copy(b, True).start()

        @pl.when(jnp.logical_not(is_mid))
        def _():
            up_copy(b, False).start()

    def up_end(s, carry):
        b = block_of(s)
        half[b] = term[b].astype(BF)
        send_up(b)
        return carry

    def up_pass(s):
        b = block_of(s)
        up_copy(b, False).wait_recv()
        half[b] = (term[b] + from_outer[b].astype(F32)).astype(BF)
        send_up(b)

    def down(s, forward):
        b = block_of(s)
        up_copy(b, True).wait_recv()

        @pl.when(is_mid)
        def _():
            from_inner[b] = (half[b].astype(F32) + from_inner[b].astype(F32)).astype(BF)

        if forward:
            down_copy(b).start()
        out_copy(b).start()

    store_term(1, slice(0, rows * width), g_own)

    @pl.when(is_end)
    def _():
        lax.fori_loop(0, NC * NC, up_end, 0)

    def side(e_side, halo, g_side, there, copy, ids_region, row_at, k, base):
        @pl.when(there)
        def _():
            copy().wait_recv()
            for i in range(HB):
                e_side[i] = placed(
                    halo[i, 0],
                    halo[i, 1],
                    pc_ref[ids_region, 0, (rows - HB + i) if k == 1 else i, 0],
                    pc_ref[ids_region, 0, (rows - HB + i) if k == 1 else i, 1],
                )

        @pl.when(jnp.logical_not(there))
        def _():
            e_side[...] = jnp.zeros_like(e_side)

        for i in range(HB):
            col = jnp.clip(ac_ref[0, 0, row_at + i, k] - base, 0, HB - 1)
            res = jnp.dot(a_v[row_at + i, k], e_side[col], preferred_element_type=F32)
            g_side[i * width : (i + 1) * width, :] = res.astype(BF)

    side(
        e_hi, halo_hi, g_hi, jnp.logical_not(last), to_previous,
        jnp.minimum(region + 1, regions - 1), rows - HB, slots - 1, rows + HB,
    )
    store_term(2, slice((rows - HB) * width, rows * width), g_hi)
    side(
        e_lo, halo_lo, g_lo, jnp.logical_not(first), to_next,
        jnp.maximum(region - 1, 0), 0, 1, 0,
    )
    store_term(0, slice(0, HB * width), g_lo)

    @pl.when(is_end)
    def _():
        lax.fori_loop(NC * NC, count, up_end, 0)

        def step(s, carry):
            down(s, False)
            return carry

        lax.fori_loop(0, count, step, 0)

    @pl.when(has_outer)
    def _():
        def head(s, carry):
            up_pass(s)
            return carry

        def steady(s, carry):
            up_pass(s)
            down(s - LAG, True)
            return carry

        def tail(s, carry):
            down(s, True)
            return carry

        lax.fori_loop(0, LAG, head, 0)
        lax.fori_loop(LAG, count, steady, 0)
        lax.fori_loop(count - LAG, count, tail, 0)

        def sent(b, carry):
            down_copy(b).wait_send()
            return carry

        lax.fori_loop(0, count, sent, 0)

    def drain(b, carry):
        up_copy(b, False).wait_send()
        out_copy(b).wait()
        return carry

    lax.fori_loop(0, count, drain, 0)

    @pl.when(jnp.logical_not(last))
    def _():
        to_next().wait_send()

    @pl.when(jnp.logical_not(first))
    def _():
        to_previous().wait_send()


def body(regions, members, a_blocks, a_cols, p_blocks, p_cols):
    rows, slots = a_blocks.shape[2:4]
    p_slots = p_blocks.shape[3]
    width = a_blocks.shape[-1]
    wide = NC * width
    band = 3 * NC
    count = NC * band
    dma = pltpu.SemaphoreType.DMA
    out = pl.pallas_call(
        functools.partial(kernel, regions, members),
        out_shape=jax.ShapeDtypeStruct((count, width, width), BF),
        in_specs=[
            pl.BlockSpec(memory_space=pl.ANY),
            pl.BlockSpec(memory_space=pltpu.SMEM),
            pl.BlockSpec(memory_space=pl.ANY),
            pl.BlockSpec(memory_space=pltpu.SMEM),
        ],
        out_specs=pl.BlockSpec(memory_space=pl.ANY),
        scratch_shapes=[
            pltpu.VMEM((rows, slots, width, width), BF),
            pltpu.VMEM((rows, p_slots, width, width), BF),
            pltpu.VMEM((HB, p_slots, width, width), BF),
            pltpu.VMEM((HB, p_slots, width, width), BF),
            pltpu.VMEM((rows, width, wide), BF),
            pltpu.VMEM((HB, width, wide), BF),
            pltpu.VMEM((HB, width, wide), BF),
            pltpu.VMEM((wide, rows * width), BF),
            pltpu.VMEM((rows * width, wide), BF),
            pltpu.VMEM((HB * width, wide), BF),
            pltpu.VMEM((HB * width, wide), BF),
            pltpu.VMEM((count, width, width), F32),
            pltpu.VMEM((count, width, width), BF),
            pltpu.VMEM((count, width, width), BF),
            pltpu.VMEM((count, width, width), BF),
            dma((rows // GROUP,)),
            dma,
            dma,
            dma,
            dma,
            dma,
            dma((count,)),
            dma((count,)),
            dma((count,)),
            dma((count,)),
            dma((count,)),
        ],
        compiler_params=pltpu.CompilerParams(
            collective_id=0, has_side_effects=True, vmem_limit_bytes=48 * 1024 * 1024
        ),
        cost_estimate=pl.CostEstimate(
            flops=2_000_000_000, bytes_accessed=5_000_000, transcendentals=0
        ),
    )(a_blocks, a_cols, p_blocks, p_cols)
    return out.reshape(NC, band, width, width).transpose(2, 0, 1, 3)[None]


def solution(mesh):
    return jax.shard_map(
        functools.partial(body, mesh.shape["agg"], mesh.shape["grp"]),
        mesh=mesh,
        in_specs=(
            P("agg", "grp", None, None, None, None),
            P("agg", "grp", None, None),
            P("agg", "grp", None, None, None, None),
            P(None, "grp", None, None),
        ),
        out_specs=P("agg", None, None, None, None),
        check_vma=False,
    )
```

time: 127 us -> 45.3 us (0.36)
  waiting for transfers between devices: 51.5 us -> 0 us
  Pallas kernels: 0 us -> 39.4 us
  matrix products: 28.8 us -> 0 us
  local copies, waits for them, and re-layouts: 26.8 us -> 5.45 us
  between operations: 13.5 us -> 0.01 us
  starting transfers between devices: 3.67 us -> 0 us
  other arithmetic: 1.77 us -> 0 us
    psum x1 -> x0, waiting for transfers between devices: 51.4 us -> none  [body(): summed = lax.psum(term.astype(jnp.bfloat16), 'grp')]
    pallas_call x0 -> x1, Pallas kernels: none -> 39.4 us  [body(): pl.pallas_call(functools.partial(kernel, regions, members), out_shape=jax...]
    dot_general x8 -> x0, matrix products: 28.8 us -> none  [the longest x1 7.05 us: body(): jnp.einsum('rcxy,rdxz->ycdz', p_routed, grouped_high, preferred_element_t...]
    reshape x1 -> x0, local copies, waits for them, and re-layouts: 12.8 us -> none  [body(): applied = applied.reshape(row_count, a_slots * p_slots, width, width)]
    unnamed x4 -> x7, local copies, waits for them, and re-layouts: 0.01 us -> 5.45 us
    dynamic_update_slice x4 -> x0, local copies, waits for them, and re-layouts: 4.78 us -> none  [body(): lax.map(product_group, (a_local.reshape(group_count, group_rows, a_slots,...]
    gather x5 -> x0, local copies, waits for them, and re-layouts: 3.8 us -> none  [the longest x4 3.19 us: product_group(): taken = p_extended[col_group]]
    ppermute x2 -> x0, starting transfers between devices: 3.66 us -> none  [the longest x1 2.37 us: with_halo(): lax.ppermute(lax.slice_in_dim(block, block.shape[dim] - width, None, axis...]
  transfers between devices with their start and end apart: 3 -> 0, of which waited for: 1 -> 0; matrix products, arithmetic and copies ran while one was open for 7% -> 0% of each run, Pallas kernels for 0% -> 0%
where the time goes in v1:
time: 45.3 us; the launch traced here: 44.9 us
  Pallas kernels  39.4 us (87%)
  local copies, waits for them, and re-layouts  5.45 us (12%)
    pallas_call x1, Pallas kernels, body(): pl.pallas_call(functools.partial(kernel, regions, members), out_shape=jax...  39.4 us
    unnamed x7, local copies, waits for them, and re-layouts  5.45 us

profile of v1, /device:TPU:0, one launch (start us, length us, event | category | flops | bytes accessed | tf_op | source)
XLA Modules:
  0.0 44.9 jit_solution(1818337874191210781)
XLA Ops:
  0.0 0.8 %copy.5.ac_ref = s32[1,1,16,5]{3,2,1,0:T(8,128)S(1)} copy(s32[1,1,16,5]{2,1,3,0:T(1,128)} %param.5) | data formatting | bytes 640 | tf_op args[1]
  0.8 0.8 %copy.6.pc_ref = s32[8,1,16,2]{3,2,1,0:T(8,128)S(1)} copy(s32[8,1,16,2]{2,3,1,0:T(2,128)} %param.7) | data formatting | bytes 2048 | tf_op args[3]
  1.6 0.0 copy-start
  1.6 1.7 %copy-done = bf16[1,1,16,5,128,128]{5,4,3,2,1,0:T(8,128)(2,1)S(1)} copy-done((bf16[1,1,16,5,128,128]{5,4,3,2,1,0:T(8,128)(2,1)S(1)}, bf16[1,1,16,5,128,128]{5,4,3,2,1,0:T(8,128)(2,1)}, u32[]{:S(2)}) %copy-start) | copy-done | bytes 2621464
  3.3 0.0 copy-start.1
  3.3 1.2 %copy-done.1 = bf16[1,1,16,2,128,128]{5,4,3,2,1,0:T(8,128)(2,1)S(1)} copy-done((bf16[1,1,16,2,128,128]{5,4,3,2,1,0:T(8,128)(2,1)S(1)}, bf16[1,1,16,2,128,128]{5,4,3,2,1,0:T(8,128)(2,1)}, u32[]{:S(2)}) %copy-start.1) | copy-done | bytes 1048600
  4.5 39.4 %shard_map.46 = bf16[27,128,128]{2,1,0:T(8,128)(2,1)S(1)} custom-call(bf16[1,1,16,5,128,128]{5,4,3,2,1,0:T(8,128)(2,1)S(1)} %copy-done, s32[1,1,16,5]{3,2,1,0:T(8,128)S(1)} %copy.5.ac_ref, bf16[1,1,16,2,128,128]{5,4,3,2,1,0:T(8,128)(2,1)S(1)} %copy-done.1, s32[8,1,16,2]{3,2,1,0:T(8,128)S(1)} %copy.6.pc_ref), custom_call_target="tpu_custom_call" | custom-call | flops 2000000000 | bytes 5000000 | tf_op jit(solution)/shard_map/pallas_call | solution.py:338
  44.0 0.9 %copy.8 = bf16[1,128,3,9,128]{4,1,3,2,0:T(8,128)(2,1)} copy(bf16[1,128,3,9,128]{4,1,3,2,0:T(8,128)(2,1)S(1)} %bitcast.5) | data formatting | bytes 1769472
Async XLA Ops:
  1.6 1.7 %copy-start = (bf16[1,1,16,5,128,128]{5,4,3,2,1,0:T(8,128)(2,1)S(1)}, bf16[1,1,16,5,128,128]{5,4,3,2,1,0:T(8,128)(2,1)}, u32[]{:S(2)}) copy-start(bf16[1,1,16,5,128,128]{5,4,3,2,1,0:T(8,128)(2,1)} %a_ref.1) | copy-start | bytes 7864324
  3.3 1.2 %copy-start.1 = (bf16[1,1,16,2,128,128]{5,4,3,2,1,0:T(8,128)(2,1)S(1)}, bf16[1,1,16,2,128,128]{5,4,3,2,1,0:T(8,128)(2,1)}, u32[]{:S(2)}) copy-start(bf16[1,1,16,2,128,128]{5,4,3,2,1,0:T(8,128)(2,1)} %p_ref.1) | copy-start | bytes 3145732

commit v2 on v1

--- a/solution.py
+++ b/solution.py
@@ -90,6 +90,21 @@
     greet(jnp.logical_not(last), region + 1, g)
     greet(has_outer, region, outer)
     greet(jnp.bool_(True), region, inner)
+    def place(block_0, block_1, id_0, id_1, c):
+        zero = jnp.zeros_like(block_0)
+        return jnp.where(id_0 == c, block_0, jnp.where(id_1 == c, block_1, zero))
+
+    p_copy.wait()
+
+    def build(r, carry):
+        for c in range(NC):
+            e_own[c, r] = place(
+                p_v[r, 0], p_v[r, 1], pc_ref[region, 0, 0, r], pc_ref[region, 0, 1, r], c
+            )
+        return carry
+
+    lax.fori_loop(0, rows, build, 0, unroll=4)
+
     pl.semaphore_wait(
         barrier,
         1
@@ -126,48 +141,43 @@
     def _():
         to_previous().start()
 
-    def placed(block_0, block_1, id_0, id_1):
-        zero = jnp.zeros_like(block_0)
-        return jnp.concatenate(
-            [
-                jnp.where(id_0 == c, block_0, jnp.where(id_1 == c, block_1, zero))
-                for c in range(NC)
-            ],
-            axis=1,
-        )
-
-    p_copy.wait()
-
-    def build(r, carry):
-        row = placed(p_v[r, 0], p_v[r, 1], pc_ref[region, 0, r, 0], pc_ref[region, 0, r, 1])
-        e_own[r] = row
-        et[:, pl.ds(pl.multiple_of(r * width, width), width)] = row.T
-        return carry
-
-    lax.fori_loop(0, rows, build, 0, unroll=4)
-
-    def multiply(i, carry):
-        a_copy(i).wait()
-        for j in range(GROUP):
-            r = i * GROUP + j
-            pieces = []
-            for k in range(slots):
-                col = jnp.clip(ac_ref[0, 0, r, k] - HB, 0, rows - 1)
-                piece = e_own[col]
-                if k == 1:
-                    keep = jnp.logical_or(first, i > 0)
-                    piece = jnp.where(keep, piece, jnp.zeros_like(piece))
-                if k == slots - 1:
-                    keep = jnp.logical_or(last, i < rows // GROUP - 1)
-                    piece = jnp.where(keep, piece, jnp.zeros_like(piece))
-                pieces.append(piece)
-            lhs = jnp.concatenate([a_v[r, k] for k in range(slots)], axis=1)
-            rhs = jnp.concatenate(pieces, axis=0)
-            res = jnp.dot(lhs, rhs, preferred_element_type=F32)
-            g_own[pl.ds(pl.multiple_of(r * width, width), width), :] = res.astype(BF)
-        return carry
-
-    lax.fori_loop(0, rows // GROUP, multiply, 0)
+    def multiply(q):
+        def step(i, carry):
+            if q == 0:
+                a_copy(i).wait()
+            for j in range(GROUP):
+                r = i * GROUP + j
+                here = pl.ds(pl.multiple_of(r * width, width), width)
+                pieces = []
+                for k in range(slots):
+                    col = jnp.clip(ac_ref[0, k, 0, r] - HB, 0, rows - 1)
+                    piece = e_own[q, col]
+                    if k == 1:
+                        keep = jnp.logical_or(first, i > 0)
+                        piece = jnp.where(keep, piece, jnp.zeros_like(piece))
+                    if k == slots - 1:
+                        keep = jnp.logical_or(last, i < rows // GROUP - 1)
+                        piece = jnp.where(keep, piece, jnp.zeros_like(piece))
+                    pieces.append(piece)
+                lhs = jnp.concatenate([a_v[r, k] for k in range(slots)], axis=1)
+                rhs = jnp.concatenate(pieces, axis=0)
+                res = jnp.dot(lhs, rhs, preferred_element_type=F32)
+                g_own[q, here, :] = res.astype(BF)
+                if q == 0:
+                    turned_0 = p_v[r, 0].T
+                    turned_1 = p_v[r, 1].T
+                    for c in range(NC):
+                        et[c * width : (c + 1) * width, here] = place(
+                            turned_0, turned_1, pc_ref[region, 0, 0, r], pc_ref[region, 0, 1, r], c
+                        )
+            return carry
+
+        lax.fori_loop(0, rows // GROUP, step, 0)
+
+    def own_term(q):
+        res = jnp.dot(et[...], g_own[q], preferred_element_type=F32)
+        for c in range(NC):
+            term[c * band + NC + q] = res[c * width : (c + 1) * width]
 
     def store_term(part, lhs_cols, rhs):
         for c in range(NC):
@@ -180,7 +190,7 @@
     def block_of(s):
         part = (s // (NC * NC) + 1) % 3
         i = s % (NC * NC)
-        return (i // NC) * band + part * NC + i % NC
+        return (i % NC) * band + part * NC + i // NC
 
     def up_copy(b, middle):
         return pltpu.make_async_remote_copy(
@@ -238,48 +248,73 @@
             down_copy(b).start()
         out_copy(b).start()
 
-    store_term(1, slice(0, rows * width), g_own)
-
-    @pl.when(is_end)
-    def _():
-        lax.fori_loop(0, NC * NC, up_end, 0)
-
     def side(e_side, halo, g_side, there, copy, ids_region, row_at, k, base):
         @pl.when(there)
         def _():
             copy().wait_recv()
             for i in range(HB):
-                e_side[i] = placed(
-                    halo[i, 0],
-                    halo[i, 1],
-                    pc_ref[ids_region, 0, (rows - HB + i) if k == 1 else i, 0],
-                    pc_ref[ids_region, 0, (rows - HB + i) if k == 1 else i, 1],
-                )
+                at = (rows - HB + i) if k == 1 else i
+                id_0, id_1 = pc_ref[ids_region, 0, 0, at], pc_ref[ids_region, 0, 1, at]
+                for c in range(NC):
+                    e_side[i, :, c * width : (c + 1) * width] = place(
+                        halo[i, 0], halo[i, 1], id_0, id_1, c
+                    )
 
         @pl.when(jnp.logical_not(there))
         def _():
             e_side[...] = jnp.zeros_like(e_side)
 
         for i in range(HB):
-            col = jnp.clip(ac_ref[0, 0, row_at + i, k] - base, 0, HB - 1)
+            col = jnp.clip(ac_ref[0, k, 0, row_at + i] - base, 0, HB - 1)
             res = jnp.dot(a_v[row_at + i, k], e_side[col], preferred_element_type=F32)
             g_side[i * width : (i + 1) * width, :] = res.astype(BF)
 
+    def end_up(start, stop):
+        @pl.when(is_end)
+        def _():
+            lax.fori_loop(start, stop, up_end, 0)
+
+    def middle_pass(start, stop, lag):
+        @pl.when(has_outer)
+        def _():
+            def step(s, carry):
+                up_pass(s)
+                if lag:
+                    down(s - lag, True)
+                return carry
+
+            lax.fori_loop(start, stop, step, 0)
+
+    own = NC * NC
+    multiply(0)
+    own_term(0)
+    end_up(0, NC)
+    multiply(1)
+    middle_pass(0, NC, 0)
+    own_term(1)
+    end_up(NC, 2 * NC)
+    multiply(2)
+    middle_pass(NC, 2 * NC, 0)
+    own_term(2)
+    end_up(2 * NC, own)
+    middle_pass(2 * NC, own, 2 * NC)
     side(
         e_hi, halo_hi, g_hi, jnp.logical_not(last), to_previous,
         jnp.minimum(region + 1, regions - 1), rows - HB, slots - 1, rows + HB,
     )
     store_term(2, slice((rows - HB) * width, rows * width), g_hi)
+    end_up(own, 2 * own)
+    middle_pass(own, own + NC, 2 * NC)
     side(
         e_lo, halo_lo, g_lo, jnp.logical_not(first), to_next,
         jnp.maximum(region - 1, 0), 0, 1, 0,
     )
     store_term(0, slice(0, HB * width), g_lo)
+    end_up(2 * own, count)
+    middle_pass(own + NC, own + NC + 1, 2 * NC)
 
     @pl.when(is_end)
     def _():
-        lax.fori_loop(NC * NC, count, up_end, 0)
-
         def step(s, carry):
             down(s, False)
             return carry
@@ -288,22 +323,21 @@
 
     @pl.when(has_outer)
     def _():
-        def head(s, carry):
-            up_pass(s)
+        at = own + NC + 1
+
+        def catch_up(s, carry):
+            down(s, True)
             return carry
+
+        lax.fori_loop(at - 2 * NC, at - LAG, catch_up, 0)
 
         def steady(s, carry):
             up_pass(s)
             down(s - LAG, True)
             return carry
 
-        def tail(s, carry):
-            down(s, True)
-            return carry
-
-        lax.fori_loop(0, LAG, head, 0)
-        lax.fori_loop(LAG, count, steady, 0)
-        lax.fori_loop(count - LAG, count, tail, 0)
+        lax.fori_loop(at, count, steady, 0)
+        lax.fori_loop(count - LAG, count, catch_up, 0)
 
         def sent(b, carry):
             down_copy(b).wait_send()
@@ -339,9 +373,9 @@
         functools.partial(kernel, regions, members),
         out_shape=jax.ShapeDtypeStruct((count, width, width), BF),
         in_specs=[
-            pl.BlockSpec(memory_space=pl.ANY),
+            pl.BlockSpec(memory_space=pltpu.HBM),
             pl.BlockSpec(memory_space=pltpu.SMEM),
-            pl.BlockSpec(memory_space=pl.ANY),
+            pl.BlockSpec(memory_space=pltpu.HBM),
             pl.BlockSpec(memory_space=pltpu.SMEM),
         ],
         out_specs=pl.BlockSpec(memory_space=pl.ANY),
@@ -350,11 +384,11 @@
             pltpu.VMEM((rows, p_slots, width, width), BF),
             pltpu.VMEM((HB, p_slots, width, width), BF),
             pltpu.VMEM((HB, p_slots, width, width), BF),
-            pltpu.VMEM((rows, width, wide), BF),
+            pltpu.VMEM((NC, rows, width, width), BF),
             pltpu.VMEM((HB, width, wide), BF),
             pltpu.VMEM((HB, width, wide), BF),
             pltpu.VMEM((wide, rows * width), BF),
-            pltpu.VMEM((rows * width, wide), BF),
+            pltpu.VMEM((NC, rows * width, width), BF),
             pltpu.VMEM((HB * width, wide), BF),
             pltpu.VMEM((HB * width, wide), BF),
             pltpu.VMEM((count, width, width), F32),
@@ -374,12 +408,12 @@
             dma((count,)),
         ],
         compiler_params=pltpu.CompilerParams(
-            collective_id=0, has_side_effects=True, vmem_limit_bytes=48 * 1024 * 1024
+            collective_id=0, has_side_effects=True, vmem_limit_bytes=60 * 1024 * 1024
         ),
         cost_estimate=pl.CostEstimate(
             flops=2_000_000_000, bytes_accessed=5_000_000, transcendentals=0
         ),
-    )(a_blocks, a_cols, p_blocks, p_cols)
+    )(a_blocks, a_cols.transpose(0, 3, 1, 2), p_blocks, p_cols.transpose(0, 1, 3, 2))
     return out.reshape(NC, band, width, width).transpose(2, 0, 1, 3)[None]
 
 

time: 45.3 us -> 39.9 us (0.88)
  local copies, waits for them, and re-layouts: 5.45 us -> 2.17 us
  Pallas kernels: 39.4 us -> 37.5 us
    unnamed x7 -> x1, local copies, waits for them, and re-layouts: 5.45 us -> 2.17 us
    pallas_call x1, Pallas kernels: 39.4 us -> 37.5 us  [body(): pl.pallas_call(functools.partial(kernel, regions, members), out_shape=jax...]
where the time goes in v2:
time: 39.9 us; the launch traced here: 39.7 us
  Pallas kernels  37.5 us (94%)
  local copies, waits for them, and re-layouts  2.17 us (5%)
    pallas_call x1, Pallas kernels, body(): pl.pallas_call(functools.partial(kernel, regions, members), out_shape=jax...  37.5 us
    unnamed x1, local copies, waits for them, and re-layouts  2.17 us

profile of v2, /device:TPU:0, one launch (start us, length us, event | category | flops | bytes accessed | tf_op | source)
XLA Modules:
  0.0 39.7 jit_solution(5611237162785096514)
XLA Ops:
  0.0 37.5 %shard_map.46 = bf16[27,128,128]{2,1,0:T(8,128)(2,1)} custom-call(bf16[1,1,16,5,128,128]{5,4,3,2,1,0:T(8,128)(2,1)} %a_ref.1, s32[1,5,1,16]{3,2,1,0:T(1,128)} %bitcast.9, bf16[1,1,16,2,128,128]{5,4,3,2,1,0:T(8,128)(2,1)} %p_ref.1, s32[8,1,2,16]{3,2,1,0:T(2,128)} %bitcast.8), custom_call_target="tpu_custom_call" | custom-call | flops 2000000000 | bytes 5000000 | tf_op jit(solution)/shard_map/pallas_call | solution.py:372
  37.5 2.2 %copy.6 = bf16[1,128,3,9,128]{4,1,3,2,0:T(8,128)(2,1)} copy(bf16[1,128,3,9,128]{4,1,3,2,0:T(8,128)(2,1)} %bitcast.7) | data formatting | bytes 1769472

commit v3 on v2

--- a/solution.py
+++ b/solution.py
@@ -9,7 +9,7 @@
 
 NC = 3
 HB = 4
-LAG = 4
+LAG = 3
 GROUP = 4
 MESH = pl.DeviceIdType.MESH
 BF = jnp.bfloat16
@@ -141,38 +141,33 @@
     def _():
         to_previous().start()
 
-    def multiply(q):
-        def step(i, carry):
-            if q == 0:
+    def multiply(q, opening, between):
+        for i in range(rows // GROUP):
+            if opening:
                 a_copy(i).wait()
-            for j in range(GROUP):
-                r = i * GROUP + j
-                here = pl.ds(pl.multiple_of(r * width, width), width)
+            for r in range(i * GROUP, (i + 1) * GROUP):
+                here = slice(r * width, (r + 1) * width)
                 pieces = []
                 for k in range(slots):
                     col = jnp.clip(ac_ref[0, k, 0, r] - HB, 0, rows - 1)
                     piece = e_own[q, col]
-                    if k == 1:
-                        keep = jnp.logical_or(first, i > 0)
-                        piece = jnp.where(keep, piece, jnp.zeros_like(piece))
-                    if k == slots - 1:
-                        keep = jnp.logical_or(last, i < rows // GROUP - 1)
-                        piece = jnp.where(keep, piece, jnp.zeros_like(piece))
+                    if k == 1 and r < HB:
+                        piece = jnp.where(first, piece, jnp.zeros_like(piece))
+                    if k == slots - 1 and r >= rows - HB:
+                        piece = jnp.where(last, piece, jnp.zeros_like(piece))
                     pieces.append(piece)
                 lhs = jnp.concatenate([a_v[r, k] for k in range(slots)], axis=1)
                 rhs = jnp.concatenate(pieces, axis=0)
                 res = jnp.dot(lhs, rhs, preferred_element_type=F32)
                 g_own[q, here, :] = res.astype(BF)
-                if q == 0:
+                if opening:
                     turned_0 = p_v[r, 0].T
                     turned_1 = p_v[r, 1].T
                     for c in range(NC):
                         et[c * width : (c + 1) * width, here] = place(
                             turned_0, turned_1, pc_ref[region, 0, 0, r], pc_ref[region, 0, 1, r], c
                         )
-            return carry
-
-        lax.fori_loop(0, rows // GROUP, step, 0)
+            between()
 
     def own_term(q):
         res = jnp.dot(et[...], g_own[q], preferred_element_type=F32)
@@ -188,9 +183,7 @@
                 term[c * band + part * NC + d] = res[:, d * width : (d + 1) * width]
 
     def block_of(s):
-        part = (s // (NC * NC) + 1) % 3
-        i = s % (NC * NC)
-        return (i % NC) * band + part * NC + i // NC
+        return (s % NC) * band + (s // NC + 2 * NC - 1) % band
 
     def up_copy(b, middle):
         return pltpu.make_async_remote_copy(
@@ -274,44 +267,44 @@
         def _():
             lax.fori_loop(start, stop, up_end, 0)
 
-    def middle_pass(start, stop, lag):
+    passed = [0]
+
+    def middle_pass():
+        at = passed[0]
+        passed[0] += 1
+
         @pl.when(has_outer)
         def _():
-            def step(s, carry):
-                up_pass(s)
-                if lag:
-                    down(s - lag, True)
-                return carry
-
-            lax.fori_loop(start, stop, step, 0)
+            up_pass(at)
+            if at >= LAG:
+                down(at - LAG, True)
 
     own = NC * NC
-    multiply(0)
-    own_term(0)
+    multiply(NC - 1, True, lambda: None)
+    own_term(NC - 1)
     end_up(0, NC)
-    multiply(1)
-    middle_pass(0, NC, 0)
-    own_term(1)
-    end_up(NC, 2 * NC)
-    multiply(2)
-    middle_pass(NC, 2 * NC, 0)
-    own_term(2)
-    end_up(2 * NC, own)
-    middle_pass(2 * NC, own, 2 * NC)
     side(
         e_hi, halo_hi, g_hi, jnp.logical_not(last), to_previous,
         jnp.minimum(region + 1, regions - 1), rows - HB, slots - 1, rows + HB,
     )
+    middle_pass()
     store_term(2, slice((rows - HB) * width, rows * width), g_hi)
-    end_up(own, 2 * own)
-    middle_pass(own, own + NC, 2 * NC)
+    end_up(NC, NC + own)
+    middle_pass()
+    middle_pass()
     side(
         e_lo, halo_lo, g_lo, jnp.logical_not(first), to_next,
         jnp.maximum(region - 1, 0), 0, 1, 0,
     )
+    middle_pass()
     store_term(0, slice(0, HB * width), g_lo)
-    end_up(2 * own, count)
-    middle_pass(own + NC, own + NC + 1, 2 * NC)
+    end_up(NC + own, NC + 2 * own)
+    middle_pass()
+    for q in range(NC - 1):
+        multiply(q, False, middle_pass)
+        own_term(q)
+        end_up(NC + 2 * own + q * NC, 2 * NC + 2 * own + q * NC)
+        middle_pass()
 
     @pl.when(is_end)
     def _():
@@ -323,21 +316,17 @@
 
     @pl.when(has_outer)
     def _():
-        at = own + NC + 1
-
-        def catch_up(s, carry):
-            down(s, True)
-            return carry
-
-        lax.fori_loop(at - 2 * NC, at - LAG, catch_up, 0)
-
         def steady(s, carry):
             up_pass(s)
             down(s - LAG, True)
             return carry
 
-        lax.fori_loop(at, count, steady, 0)
-        lax.fori_loop(count - LAG, count, catch_up, 0)
+        def tail(s, carry):
+            down(s, True)
+            return carry
+
+        lax.fori_loop(passed[0], count, steady, 0)
+        lax.fori_loop(count - LAG, count, tail, 0)
 
         def sent(b, carry):
             down_copy(b).wait_send()
@@ -371,14 +360,14 @@
     dma = pltpu.SemaphoreType.DMA
     out = pl.pallas_call(
         functools.partial(kernel, regions, members),
-        out_shape=jax.ShapeDtypeStruct((count, width, width), BF),
+        out_shape=pltpu.VMEM((count, width, width), BF),
         in_specs=[
             pl.BlockSpec(memory_space=pltpu.HBM),
             pl.BlockSpec(memory_space=pltpu.SMEM),
             pl.BlockSpec(memory_space=pltpu.HBM),
             pl.BlockSpec(memory_space=pltpu.SMEM),
         ],
-        out_specs=pl.BlockSpec(memory_space=pl.ANY),
+        out_specs=pl.BlockSpec(memory_space=pltpu.VMEM),
         scratch_shapes=[
             pltpu.VMEM((rows, slots, width, width), BF),
             pltpu.VMEM((rows, p_slots, width, width), BF),
@@ -408,7 +397,7 @@
             dma((count,)),
         ],
         compiler_params=pltpu.CompilerParams(
-            collective_id=0, has_side_effects=True, vmem_limit_bytes=60 * 1024 * 1024
+            collective_id=0, has_side_effects=True, vmem_limit_bytes=57 * 1024 * 1024
         ),
         cost_estimate=pl.CostEstimate(
             flops=2_000_000_000, bytes_accessed=5_000_000, transcendentals=0

time: 39.9 us -> 42 us (1.053)
  Pallas kernels: 37.5 us -> 40.8 us
  local copies, waits for them, and re-layouts: 2.17 us -> 0.91 us
    pallas_call x1, Pallas kernels: 37.5 us -> 40.8 us  [body(): pl.pallas_call(functools.partial(kernel, regions, members), out_shape=plt...]
    unnamed x1, local copies, waits for them, and re-layouts: 2.17 us -> 0.91 us
where the time goes in v3:
time: 42 us; the launch traced here: 41.7 us
  Pallas kernels  40.8 us (97%)
  local copies, waits for them, and re-layouts  0.91 us (2%)
    pallas_call x1, Pallas kernels, body(): pl.pallas_call(functools.partial(kernel, regions, members), out_shape=plt...  40.8 us
    unnamed x1, local copies, waits for them, and re-layouts  0.91 us

profile of v3, /device:TPU:0, one launch (start us, length us, event | category | flops | bytes accessed | tf_op | source)
XLA Modules:
  0.0 41.7 jit_solution(5955760742899019764)
XLA Ops:
  0.0 40.8 %shard_map.46 = bf16[27,128,128]{2,1,0:T(8,128)(2,1)S(1)} custom-call(bf16[1,1,16,5,128,128]{5,4,3,2,1,0:T(8,128)(2,1)} %a_ref.1, s32[1,5,1,16]{3,2,1,0:T(1,128)} %bitcast.9, bf16[1,1,16,2,128,128]{5,4,3,2,1,0:T(8,128)(2,1)} %p_ref.1, s32[8,1,2,16]{3,2,1,0:T(2,128)} %bitcast.8), custom_call_target="tpu_custom_call" | custom-call | flops 2000000000 | bytes 5000000 | tf_op jit(solution)/shard_map/pallas_call | solution.py:361
  40.8 0.9 %copy.6 = bf16[1,128,3,9,128]{4,1,3,2,0:T(8,128)(2,1)} copy(bf16[1,128,3,9,128]{4,1,3,2,0:T(8,128)(2,1)S(1)} %bitcast.7) | data formatting | bytes 1769472

commit v4 on v3

--- a/solution.py
+++ b/solution.py
@@ -113,33 +113,35 @@
         + jnp.logical_not(last).astype(jnp.int32),
     )
 
-    def to_next():
+    def to_next(i):
         return pltpu.make_async_remote_copy(
-            src_ref=p_ref.at[0, 0, pl.ds(rows - HB, HB)],
-            dst_ref=halo_lo,
-            send_sem=lo_send,
-            recv_sem=lo_recv,
+            src_ref=p_ref.at[0, 0, rows - HB + i],
+            dst_ref=halo_lo.at[i],
+            send_sem=lo_send.at[i],
+            recv_sem=lo_recv.at[i],
             device_id=(region + 1, g),
             device_id_type=MESH,
         )
 
-    def to_previous():
+    def to_previous(i):
         return pltpu.make_async_remote_copy(
-            src_ref=p_ref.at[0, 0, pl.ds(0, HB)],
-            dst_ref=halo_hi,
-            send_sem=hi_send,
-            recv_sem=hi_recv,
+            src_ref=p_ref.at[0, 0, i],
+            dst_ref=halo_hi.at[i],
+            send_sem=hi_send.at[i],
+            recv_sem=hi_recv.at[i],
             device_id=(region - 1, g),
             device_id_type=MESH,
         )
 
+    @pl.when(jnp.logical_not(first))
+    def _():
+        for i in range(HB):
+            to_previous(i).start()
+
     @pl.when(jnp.logical_not(last))
     def _():
-        to_next().start()
-
-    @pl.when(jnp.logical_not(first))
-    def _():
-        to_previous().start()
+        for i in range(HB):
+            to_next(i).start()
 
     def multiply(q, opening, between):
         for i in range(rows // GROUP):
@@ -167,7 +169,7 @@
                         et[c * width : (c + 1) * width, here] = place(
                             turned_0, turned_1, pc_ref[region, 0, 0, r], pc_ref[region, 0, 1, r], c
                         )
-            between()
+            between(i)
 
     def own_term(q):
         res = jnp.dot(et[...], g_own[q], preferred_element_type=F32)
@@ -183,7 +185,7 @@
                 term[c * band + part * NC + d] = res[:, d * width : (d + 1) * width]
 
     def block_of(s):
-        return (s % NC) * band + (s // NC + 2 * NC - 1) % band
+        return (s % NC) * band + (s // NC + NC) % band
 
     def up_copy(b, middle):
         return pltpu.make_async_remote_copy(
@@ -244,8 +246,8 @@
     def side(e_side, halo, g_side, there, copy, ids_region, row_at, k, base):
         @pl.when(there)
         def _():
-            copy().wait_recv()
             for i in range(HB):
+                copy(i).wait_recv()
                 at = (rows - HB + i) if k == 1 else i
                 id_0, id_1 = pc_ref[ids_region, 0, 0, at], pc_ref[ids_region, 0, 1, at]
                 for c in range(NC):
@@ -280,16 +282,32 @@
                 down(at - LAG, True)
 
     own = NC * NC
-    multiply(NC - 1, True, lambda: None)
-    own_term(NC - 1)
-    end_up(0, NC)
+    groups = rows // GROUP
+
+    def second(i):
+        if i >= groups - 2:
+            middle_pass()
+        if i == groups - 1:
+            middle_pass()
+
+    def third(i):
+        if i > 0:
+            middle_pass()
+
+    between = [lambda i: None, second, third]
+    for q in range(NC):
+        multiply(q, q == 0, between[q])
+        own_term(q)
+        end_up(q * NC, (q + 1) * NC)
+    middle_pass()
+    middle_pass()
     side(
         e_hi, halo_hi, g_hi, jnp.logical_not(last), to_previous,
         jnp.minimum(region + 1, regions - 1), rows - HB, slots - 1, rows + HB,
     )
     middle_pass()
     store_term(2, slice((rows - HB) * width, rows * width), g_hi)
-    end_up(NC, NC + own)
+    end_up(own, 2 * own)
     middle_pass()
     middle_pass()
     side(
@@ -298,13 +316,7 @@
     )
     middle_pass()
     store_term(0, slice(0, HB * width), g_lo)
-    end_up(NC + own, NC + 2 * own)
-    middle_pass()
-    for q in range(NC - 1):
-        multiply(q, False, middle_pass)
-        own_term(q)
-        end_up(NC + 2 * own + q * NC, 2 * NC + 2 * own + q * NC)
-        middle_pass()
+    end_up(2 * own, count)
 
     @pl.when(is_end)
     def _():
@@ -343,11 +355,13 @@
 
     @pl.when(jnp.logical_not(last))
     def _():
-        to_next().wait_send()
+        for i in range(HB):
+            to_next(i).wait_send()
 
     @pl.when(jnp.logical_not(first))
     def _():
-        to_previous().wait_send()
+        for i in range(HB):
+            to_previous(i).wait_send()
 
 
 def body(regions, members, a_blocks, a_cols, p_blocks, p_cols):
@@ -386,10 +400,10 @@
             pltpu.VMEM((count, width, width), BF),
             dma((rows // GROUP,)),
             dma,
-            dma,
-            dma,
-            dma,
-            dma,
+            dma((HB,)),
+            dma((HB,)),
+            dma((HB,)),
+            dma((HB,)),
             dma((count,)),
             dma((count,)),
             dma((count,)),

time: 42 us -> 41 us (0.976)
  Pallas kernels: 40.8 us -> 39.8 us
    pallas_call x1, Pallas kernels: 40.8 us -> 39.8 us  [body(): pl.pallas_call(functools.partial(kernel, regions, members), out_shape=plt...]
where the time goes in v4:
time: 41 us; the launch traced here: 40.7 us
  Pallas kernels  39.8 us (97%)
  local copies, waits for them, and re-layouts  0.91 us (2%)
    pallas_call x1, Pallas kernels, body(): pl.pallas_call(functools.partial(kernel, regions, members), out_shape=plt...  39.8 us
    unnamed x1, local copies, waits for them, and re-layouts  0.91 us

profile of v4, /device:TPU:0, one launch (start us, length us, event | category | flops | bytes accessed | tf_op | source)
XLA Modules:
  0.0 40.7 jit_solution(10243280653045459388)
XLA Ops:
  0.0 39.8 %shard_map.46 = bf16[27,128,128]{2,1,0:T(8,128)(2,1)S(1)} custom-call(bf16[1,1,16,5,128,128]{5,4,3,2,1,0:T(8,128)(2,1)} %a_ref.1, s32[1,5,1,16]{3,2,1,0:T(1,128)} %bitcast.9, bf16[1,1,16,2,128,128]{5,4,3,2,1,0:T(8,128)(2,1)} %p_ref.1, s32[8,1,2,16]{3,2,1,0:T(2,128)} %bitcast.8), custom_call_target="tpu_custom_call" | custom-call | flops 2000000000 | bytes 5000000 | tf_op jit(solution)/shard_map/pallas_call | solution.py:375
  39.8 0.9 %copy.6 = bf16[1,128,3,9,128]{4,1,3,2,0:T(8,128)(2,1)} copy(bf16[1,128,3,9,128]{4,1,3,2,0:T(8,128)(2,1)S(1)} %bitcast.7) | data formatting | bytes 1769472

commit v5 on v2

--- a/solution.py
+++ b/solution.py
@@ -294,24 +294,24 @@
     own_term(1)
     end_up(NC, 2 * NC)
     multiply(2)
-    middle_pass(NC, 2 * NC, 0)
+    middle_pass(NC, 2 * NC, NC)
     own_term(2)
     end_up(2 * NC, own)
-    middle_pass(2 * NC, own, 2 * NC)
+    middle_pass(2 * NC, own, NC)
     side(
         e_hi, halo_hi, g_hi, jnp.logical_not(last), to_previous,
         jnp.minimum(region + 1, regions - 1), rows - HB, slots - 1, rows + HB,
     )
     store_term(2, slice((rows - HB) * width, rows * width), g_hi)
     end_up(own, 2 * own)
-    middle_pass(own, own + NC, 2 * NC)
+    middle_pass(own, own + NC, NC)
     side(
         e_lo, halo_lo, g_lo, jnp.logical_not(first), to_next,
         jnp.maximum(region - 1, 0), 0, 1, 0,
     )
     store_term(0, slice(0, HB * width), g_lo)
     end_up(2 * own, count)
-    middle_pass(own + NC, own + NC + 1, 2 * NC)
+    middle_pass(own + NC, own + LAG, 0)
 
     @pl.when(is_end)
     def _():
@@ -323,21 +323,17 @@
 
     @pl.when(has_outer)
     def _():
-        at = own + NC + 1
-
-        def catch_up(s, carry):
-            down(s, True)
-            return carry
-
-        lax.fori_loop(at - 2 * NC, at - LAG, catch_up, 0)
-
         def steady(s, carry):
             up_pass(s)
             down(s - LAG, True)
             return carry
 
-        lax.fori_loop(at, count, steady, 0)
-        lax.fori_loop(count - LAG, count, catch_up, 0)
+        def tail(s, carry):
+            down(s, True)
+            return carry
+
+        lax.fori_loop(own + LAG, count, steady, 0)
+        lax.fori_loop(count - LAG, count, tail, 0)
 
         def sent(b, carry):
             down_copy(b).wait_send()
@@ -371,14 +367,14 @@
     dma = pltpu.SemaphoreType.DMA
     out = pl.pallas_call(
         functools.partial(kernel, regions, members),
-        out_shape=jax.ShapeDtypeStruct((count, width, width), BF),
+        out_shape=pltpu.VMEM((count, width, width), BF),
         in_specs=[
             pl.BlockSpec(memory_space=pltpu.HBM),
             pl.BlockSpec(memory_space=pltpu.SMEM),
             pl.BlockSpec(memory_space=pltpu.HBM),
             pl.BlockSpec(memory_space=pltpu.SMEM),
         ],
-        out_specs=pl.BlockSpec(memory_space=pl.ANY),
+        out_specs=pl.BlockSpec(memory_space=pltpu.VMEM),
         scratch_shapes=[
             pltpu.VMEM((rows, slots, width, width), BF),
             pltpu.VMEM((rows, p_slots, width, width), BF),
@@ -408,7 +404,7 @@
             dma((count,)),
         ],
         compiler_params=pltpu.CompilerParams(
-            collective_id=0, has_side_effects=True, vmem_limit_bytes=60 * 1024 * 1024
+            collective_id=0, has_side_effects=True, vmem_limit_bytes=57 * 1024 * 1024
         ),
         cost_estimate=pl.CostEstimate(
             flops=2_000_000_000, bytes_accessed=5_000_000, transcendentals=0

time: 39.9 us -> 39.8 us (level)
  local copies, waits for them, and re-layouts: 2.17 us -> 0.91 us
  Pallas kernels: 37.5 us -> 38.6 us
    unnamed x1, local copies, waits for them, and re-layouts: 2.17 us -> 0.91 us
    pallas_call x1, Pallas kernels: 37.5 us -> 38.6 us  [body(): pl.pallas_call(functools.partial(kernel, regions, members), out_shape=plt...]
where the time goes in v5:
time: 39.8 us; the launch traced here: 39.5 us
  Pallas kernels  38.6 us (97%)
  local copies, waits for them, and re-layouts  0.91 us (2%)
    pallas_call x1, Pallas kernels, body(): pl.pallas_call(functools.partial(kernel, regions, members), out_shape=plt...  38.6 us
    unnamed x1, local copies, waits for them, and re-layouts  0.91 us

profile of v5, /device:TPU:0, one launch (start us, length us, event | category | flops | bytes accessed | tf_op | source)
XLA Modules:
  0.0 39.5 jit_solution(9790727926740237052)
XLA Ops:
  0.0 38.6 %shard_map.46 = bf16[27,128,128]{2,1,0:T(8,128)(2,1)S(1)} custom-call(bf16[1,1,16,5,128,128]{5,4,3,2,1,0:T(8,128)(2,1)} %a_ref.1, s32[1,5,1,16]{3,2,1,0:T(1,128)} %bitcast.9, bf16[1,1,16,2,128,128]{5,4,3,2,1,0:T(8,128)(2,1)} %p_ref.1, s32[8,1,2,16]{3,2,1,0:T(2,128)} %bitcast.8), custom_call_target="tpu_custom_call" | custom-call | flops 2000000000 | bytes 5000000 | tf_op jit(solution)/shard_map/pallas_call | solution.py:368
  38.6 0.9 %copy.6 = bf16[1,128,3,9,128]{4,1,3,2,0:T(8,128)(2,1)} copy(bf16[1,128,3,9,128]{4,1,3,2,0:T(8,128)(2,1)S(1)} %bitcast.7) | data formatting | bytes 1769472
